TPU v7x, 256 devices: a whole 4x4x8 slice. The times are simulated.
256 devices in a mesh: dp: 16 (over z_hi, y), tensor: 16 (over x, z_lo, core).
Axes of the slice: x: 4, y: 4, z: 8 (z_hi: 4, z_lo: 2; z = z_hi * 2 + z_lo), core: 2. Of those that a mesh axis runs over, the one named last changes fastest.
Arguments:
- x_rows: bfloat16 [12288, 4096], P(('dp', 'tensor')), may hold values from -24 to 24
- grad_out: bfloat16 [12288, 4096], P(('dp', 'tensor')), may hold values from -24 to 24
- gate_pre: bfloat16 [12288, 14336], P('dp', 'tensor'), may hold values from -8 to 8
- up_pre: bfloat16 [12288, 14336], P('dp', 'tensor'), may hold values from -6 to 6
- down_weight: bfloat16 [14336, 4096], P('tensor', 'dp'), may hold values from -0.046875 to 0.046875
Outputs:
- grad_gate: bfloat16 [12288, 14336], P('dp', 'tensor')
- grad_up: bfloat16 [12288, 14336], P('dp', 'tensor')
- grad_down: bfloat16 [14336, 4096], P('tensor', 'dp')
- gram_input: float32 [4096, 1024], P(('tensor', 'dp'))
- gram_output: float32 [4096, 1024], P(('tensor', 'dp'))
All inputs are finite; a program needn't handle non-finite values.
Results may differ from a plain program's by a relative error of at most 0.0049.
Values may be sent and summed in bfloat16 or wider, within the bound.
A program may use at most 128 MiB of HBM per device.

v0:
```python
import math

import jax
import jax.numpy as jnp
from jax import lax
from jax.sharding import PartitionSpec as P

BLOCK = 1024


def row_gram(mine, block_cols, total):
    return (
        lax.dot_general(
            mine, block_cols, (((0,), (0,)), ((), ())), preferred_element_type=jnp.float32
        )
        / total
    )


def shards(x_rows, grad_out, gate_pre, up_pre, down_weight):
    n_tensor = lax.axis_size("tensor")
    n_data = lax.axis_size("dp")
    tensor_idx = lax.axis_index("tensor")
    data_idx = lax.axis_index("dp")
    tok_dev = x_rows.shape[0]
    width = x_rows.shape[1]
    block = BLOCK
    total = float(tok_dev * n_tensor * n_data)
    row_width = width // n_tensor
    first_row = tensor_idx * row_width
    block_start = first_row // block * block
    gate_f = gate_pre.astype(jnp.float32)
    up_f = up_pre.astype(jnp.float32)
    sigma = jax.nn.sigmoid(gate_f)
    silu = gate_f * sigma
    hidden = (silu * up_f).astype(jnp.bfloat16)
    grad_rows, input_all = (
        lax.all_gather(grad_out, "tensor", axis=0, tiled=True),
        lax.all_gather(x_rows, "tensor", axis=0, tiled=True),
    )
    in_mine = lax.dynamic_slice_in_dim(input_all, first_row, row_width, 1)
    in_block = lax.dynamic_slice_in_dim(input_all, block_start, block, 1)
    grad_hidden = lax.dot_general(
        grad_rows,
        lax.all_gather(down_weight, "dp", axis=1, tiled=True),
        (((1,), (1,)), ((), ())),
        preferred_element_type=jnp.float32,
    )
    grad_up = (grad_hidden * silu).astype(jnp.bfloat16)
    grad_gate = (grad_hidden * up_f * sigma * (1.0 + gate_f * (1.0 - sigma))).astype(jnp.bfloat16)
    scale = 1.0 / math.sqrt(total)
    partial_grad = (
        lax.dot_general(
            hidden, grad_rows, (((0,), (0,)), ((), ())), preferred_element_type=jnp.float32
        )
        * scale
    )
    grad_down = lax.psum_scatter(partial_grad, "dp", scatter_dimension=1, tiled=True).astype(
        jnp.bfloat16
    )
    gram_in_part = row_gram(in_mine, in_block, total)
    out_mine = lax.dynamic_slice_in_dim(grad_rows, first_row, row_width, 1)
    out_block = lax.dynamic_slice_in_dim(grad_rows, block_start, block, 1)
    gram_out_part = row_gram(out_mine, out_block, total)
    share = row_width // n_data
    gram_in_all, gram_out_all = lax.psum((gram_in_part, gram_out_part), "dp")
    gram_input = lax.dynamic_slice_in_dim(gram_in_all, data_idx * share, share, 0)
    gram_output = lax.dynamic_slice_in_dim(gram_out_all, data_idx * share, share, 0)
    return (grad_gate, grad_up, grad_down, gram_input, gram_output)


def solution(mesh):
    return jax.shard_map(
        shards,
        mesh=mesh,
        in_specs=(
            P(("dp", "tensor"), None),
            P(("dp", "tensor"), None),
            P("dp", "tensor"),
            P("dp", "tensor"),
            P("tensor", "dp"),
        ),
        out_specs=(
            P("dp", "tensor"),
            P("dp", "tensor"),
            P("tensor", "dp"),
            P(("tensor", "dp"), None),
            P(("tensor", "dp"), None),
        ),
        check_vma=False,
    )
```

profile of v0, /device:TPU:1, one launch (start us, length us, event | category | flops | bytes accessed | tf_op | source)
XLA Modules:
  0.0 598.9 jit_solution(13269570061533851015)
XLA Ops:
  7.2 0.0 all-gather.8.cloned.1.call-start
  7.2 0.7 all-gather.8.cloned.1.call-update
  7.9 0.0 all-gather.4.cloned.1.call-start
  7.9 0.7 all-gather.4.cloned.1.call-update
  8.6 0.0 all-gather.6.cloned.1.call-start
  8.7 0.7 all-gather.6.cloned.1.call-update
  9.4 0.0 all-reduce.3.cloned.1.call-start
  9.4 49.6 %all-gather.8.cloned.1.call-done = bf16[768,4096]{1,0:T(8,128)(2,1)} async-done(((bf16[48,4096]{1,0:T(8,128)(2,1)}), bf16[768,4096]{1,0:T(8,128)(2,1)}) %all-gather.8.cloned.1.call-update) | async-done | bytes 6291472 | tf_op jit(solution)/shard_map/all_gather | solution.py:39
  59.0 3.1 fusion.13
  62.2 0.0 copy-start
  62.2 0.0 copy-start.1
  62.2 44.4 %all-gather.4.cloned.1.call-done = bf16[768,4096]{1,0:T(8,128)(2,1)} async-done(((bf16[48,4096]{1,0:T(8,128)(2,1)}), bf16[768,4096]{1,0:T(8,128)(2,1)}) %all-gather.4.cloned.1.call-update) | async-done | bytes 6291472 | tf_op jit(solution)/shard_map/all_gather | solution.py:38
  106.6 3.1 fusion.16
  109.7 0.0 all-reduce.3.cloned.1.call-update
  109.8 0.0 reduce-scatter.2.cloned.1.call-start
  109.8 0.0 copy-done
  109.8 0.0 copy-done.1
  109.8 11.3 %convolution_multiply_fusion = f32[896,4096]{1,0:T(8,128)} fusion(bf16[768,4096]{1,0:T(8,128)(2,1)} %all-gather.4.cloned.1.call-done, bf16[768,896]{1,0:T(8,128)(2,1)S(1)} %copy-done.1, bf16[768,896]{1,0:T(8,128)(2,1)S(1)} %copy-done), kind=kOutput, calls=%fused_computation | convolution fusion | flops 5646319616 | bytes 23724032 | tf_op jit(solution)/shard_map/dot_general | solution.py:53
  121.1 0.0 reduce-scatter.2.cloned.1.call-update
  121.1 102.7 %all-gather.6.cloned.1.call-done = bf16[896,4096]{1,0:T(8,128)(2,1)} async-done(((bf16[896,256]{1,0:T(8,128)(2,1)}), bf16[896,4096]{1,0:T(8,128)(2,1)}) %all-gather.6.cloned.1.call-update) | async-done | bytes 7340048 | tf_op jit(solution)/shard_map/all_gather | solution.py:45
  223.9 12.7 %multiply_convert_fusion = (bf16[768,896]{1,0:T(8,128)(2,1)}, bf16[768,896]{1,0:T(8,128)(2,1)}) fusion(bf16[768,896]{1,0:T(8,128)(2,1)S(1)} %copy-done, bf16[768,896]{1,0:T(8,128)(2,1)S(1)} %copy-done.1, bf16[768,4096]{1,0:T(8,128)(2,1)} %all-gather.4.cloned.1.call-done, bf16[896,4096]{1,0:T(8,128)(2,1)} %all-gather.6.cloned.1.call-done), kind=kOutput, calls=%fused_computation.14 | convolution fusion | flops 5647466496 | bytes 19136512 | tf_op jit(solution)/shard_map/dot_general | solution.py:43
  236.6 159.7 %all-reduce.3.cloned.1.call-done = (f32[256,1024]{1,0:T(8,128)}, f32[256,1024]{1,0:T(8,128)}) async-done(((f32[256,1024]{1,0:T(8,128)}, f32[256,1024]{1,0:T(8,128)}), (f32[256,1024]{1,0:T(8,128)}, f32[256,1024]{1,0:T(8,128)})) %all-reduce.3.cloned.1.call-update) | async-done | bytes 2097168 | tf_op jit(solution)/shard_map/psum | solution.py:66
  396.3 1.5 constant_dynamic-slice_fusion
  397.9 192.5 %reduce-scatter.2.cloned.1.call-done = f32[896,256]{1,0:T(8,128)} async-done(((f32[896,4096]{1,0:T(8,128)}), f32[896,256]{1,0:T(8,128)}) %reduce-scatter.2.cloned.1.call-update) | async-done | bytes 917520 | tf_op jit(solution)/shard_map/reduce_scatter | solution.py:58
  590.3 2.0 convert_element_type.23
Async XLA Ops:
  7.2 51.9 %all-gather.8.cloned.1.call-start = ((), (), s32[]{:S(2)}) async-start(), calls=%async_computation.4 | async-start | bytes 6684672 | tf_op jit(solution)/shard_map/all_gather | solution.py:39
  7.9 98.7 %all-gather.4.cloned.1.call-start = ((), (), s32[]{:S(2)}) async-start(), calls=%async_computation.1 | async-start | bytes 6684672 | tf_op jit(solution)/shard_map/all_gather | solution.py:38
  8.6 215.2 %all-gather.6.cloned.1.call-start = ((), (), s32[]{:S(2)}) async-start(), calls=%async_computation.2 | async-start | bytes 7798784 | tf_op jit(solution)/shard_map/all_gather | solution.py:45
  9.4 386.9 %all-reduce.3.cloned.1.call-start = ((), (), s32[]{:S(2)}) async-start(), calls=%async_computation.5 | async-start | bytes 4194304 | tf_op jit(solution)/shard_map/psum | solution.py:66
  62.2 47.7 %copy-start = (bf16[768,896]{1,0:T(8,128)(2,1)S(1)}, bf16[768,896]{1,0:T(8,128)(2,1)}, u32[]{:S(2)}) copy-start(bf16[768,896]{1,0:T(8,128)(2,1)} %param.7) | copy-start | bytes 4128772
  62.2 47.7 %copy-start.1 = (bf16[768,896]{1,0:T(8,128)(2,1)S(1)}, bf16[768,896]{1,0:T(8,128)(2,1)}, u32[]{:S(2)}) copy-start(bf16[768,896]{1,0:T(8,128)(2,1)} %param.8) | copy-start | bytes 4128772
  109.8 480.6 %reduce-scatter.2.cloned.1.call-start = ((), (), s32[]{:S(2)}) async-start(), calls=%async_computation.3 | async-start | bytes 15597568 | tf_op jit(solution)/shard_map/reduce_scatter | solution.py:58
Sparse Core Ops, SparseCore 0:
  9.8 49.1 all-gather.7
  60.9 45.6 all-gather.3
  109.0 114.7 all-gather.5
  226.4 169.8 all-reduce.2
  399.9 190.3 reduce-scatter.1
where the time goes:
time: 599 us
  waiting for transfers between devices  551 us (92%)
  matrix products  30.3 us (5%)
  between operations  13.8 us (2%)
    reduce_scatter x1, waiting for transfers between devices, shards(): lax.psum_scatter(partial_grad, 'dp', scatter_dimension=1, tiled=True)  192 us
    psum x1, waiting for transfers between devices, shards(): gram_in_all, gram_out_all = lax.psum((gram_in_part, gram_out_part), 'dp')  160 us
    all_gather x1, waiting for transfers between devices, shards(): lax.all_gather(down_weight, 'dp', axis=1, tiled=True)  103 us
    all_gather x1, waiting for transfers between devices, shards(): lax.all_gather(x_rows, 'tensor', axis=0, tiled=True)  49.6 us
    all_gather x1, waiting for transfers between devices, shards(): lax.all_gather(grad_out, 'tensor', axis=0, tiled=True)  44.4 us
    dot_general x1, matrix products, shards(): lax.dot_general(grad_rows, lax.all_gather(down_weight, 'dp', axis=1, tile...  12.7 us
  transfers between devices with their start and end apart: 5, of which 5 were waited for; matrix products, arithmetic and copies ran while one was open for 5% of the time, Pallas kernels for 0%

commit v1 on v0

v1 whole, which is shorter than its diff:
```python
import math

import jax
import jax.numpy as jnp
from jax import lax
from jax.experimental import pallas as pl
from jax.experimental.pallas import tpu as pltpu
from jax.sharding import PartitionSpec as P

MESH = pl.DeviceIdType.MESH
BF = jnp.bfloat16
F32 = jnp.float32
BLOCK = 1024


def kernel(
    total,
    x_ref, g_ref, gate_ref, up_ref, w_ref,
    gg_ref, gu_ref, gd_ref, gi_ref, go_ref,
    src, ghalf, tok, wf, ht, xb, asnd, arcv, part, zs, z1, z2,
    snd, rcv, ghf, gp, gbs, gbr, gas, gar, gf, gzs, gz1, gz2,
    ssem, rsem,
):
    rows = g_ref.shape[0]
    ffl, kc = w_ref.shape
    n_tok = gate_ref.shape[0]
    hk = kc // 2
    hf = ffl // 2
    d = lax.axis_index("dp")
    t = lax.axis_index("tensor")
    zh, y = d // 4, d % 4
    x, zl, c = t // 4, (t // 2) % 2, t % 2
    half = ((y + 1) // 2) % 2
    s = y // 2

    sib = (d, t + 1 - 2 * c)
    zlp = (d, t + 2 - 4 * zl)
    xr = (d, ((x + 1) % 4) * 4 + t % 4)
    xl = (d, ((x + 3) % 4) * 4 + t % 4)
    xo = (d, ((x + 2) % 4) * 4 + t % 4)
    ya = (zh * 4 + 3 - y, t)
    yb = (zh * 4 + y + 1 - 2 * (y % 2), t)
    zr = (((zh + 1) % 4) * 4 + y, t)
    zb = (((zh + 3) % 4) * 4 + y, t)
    neighbours = (sib, zlp, xr, xl, xo, ya, yb, zr, zb)

    barrier = pltpu.get_barrier_semaphore()
    for n in neighbours:
        pl.semaphore_signal(barrier, inc=1, device_id=n, device_id_type=MESH)
    pl.semaphore_wait(barrier, len(neighbours))

    names = {}
    started = []

    def sem(key):
        return names.setdefault(key, len(names))

    def send(key, src_ref, dst_ref, dev):
        k = sem(key)
        cp = pltpu.make_async_remote_copy(
            src_ref=src_ref, dst_ref=dst_ref, send_sem=ssem.at[k], recv_sem=rsem.at[k],
            device_id=dev, device_id_type=MESH,
        )
        cp.start()
        started.append(cp)

    def recv(key, dst_ref, dev):
        k = sem(key)
        pltpu.make_async_remote_copy(
            src_ref=dst_ref, dst_ref=dst_ref, send_sem=ssem.at[k], recv_sem=rsem.at[k],
            device_id=dev, device_id_type=MESH,
        ).wait_recv()

    def zz(r):
        return (zh + r) % 4

    def yy_of(h, q):
        return h + q * (3 - 2 * h)

    def wpiece(r, q, p):
        return wf.at[zz(r) * 2 + q, pl.ds(p * hk, hk), :]

    def w_to_a(r, p):
        send(("wa", r, p), wpiece(r, s, p), wpiece(r, s, p), ya)

    wf[zh * 2 + s] = w_ref[...].astype(F32).T.astype(BF)
    w_to_a(0, 0)
    send(("wl", 0), wpiece(0, s, 0), wpiece(0, s, 0), zr)
    send(("wr", 1), wpiece(0, s, 1), wpiece(0, s, 1), zb)
    w_to_a(0, 1)
    send(("wl", 1), wpiece(0, s, 1), wpiece(0, s, 1), zr)
    send(("wr", 0), wpiece(0, s, 0), wpiece(0, s, 0), zb)

    for z in range(4):
        for q in range(2):
            to = pl.ds((z * 2 + q) * kc, kc)
            other = pl.multiple_of((z * 4 + yy_of(1 - half, q)) * kc, kc)
            mine = pl.multiple_of((z * 4 + yy_of(half, q)) * kc, kc)
            ghalf[:, to] = g_ref[:, pl.ds(other, kc)]
            tok[0, x, zl, c, :, to] = g_ref[:, pl.ds(mine, kc)]

    def tpiece(slot, e, xx, cc=c):
        return tok.at[slot, xx, zl if e == 0 else 1 - zl, cc]

    x_left, x_right, x_opp = (x + 3) % 4, (x + 1) % 4, (x + 2) % 4

    def t_to_x(slot, e):
        ref = tpiece(slot, e, x)
        send(("txl", slot, e), ref, ref, xr)
        send(("txr", slot, e), ref, ref, xl)
        send(("ts", slot, e, 0), ref, ref, sib)

    send("tb", ghalf, tok.at[1, x, zl, c], yb)
    t_to_x(0, 0)
    send(("tz", 0), tpiece(0, 0, x), tpiece(0, 0, x), zlp)

    src[0] = x_ref[...]
    src[1] = g_ref[...]

    def block_cols(xx):
        return pl.ds(pl.multiple_of(xx * BLOCK, BLOCK), BLOCK)

    for r, dev in ((1, xr), (3, xl), (2, xo)):
        send(("gx", r), src.at[:, :, block_cols((x + r) % 4)], xb.at[c, zl, :, x], dev)
    xb[c, zl, :, x] = src[:, :, block_cols(x)]

    ht_tile = 128

    def hidden_tile(i):
        at = pl.ds(pl.multiple_of(i * ht_tile, ht_tile), ht_tile)
        gate = gate_ref[at, :].astype(F32)
        up = up_ref[at, :].astype(F32)
        hid = (gate * jax.nn.sigmoid(gate) * up).astype(BF)
        ht[0, :, at] = hid.astype(F32).T.astype(BF)

    n_ht = n_tok // ht_tile
    for p in range(2):
        pl.loop(p * n_ht // 2, (p + 1) * n_ht // 2)(hidden_tile)
        cols = pl.ds(p * n_tok // 2, n_tok // 2)
        send(("h", p), ht.at[0, :, cols], ht.at[1, :, cols], yb)

    recv("tb", tpiece(1, 0, x), yb)
    t_to_x(1, 0)
    send(("tz", 1), tpiece(1, 0, x), tpiece(1, 0, x), zlp)

    for r, dev in ((3, xr), (1, xl), (2, xo)):
        recv(("gx", r), xb.at[c, zl, :, (x + 4 - r) % 4], dev)
    send("gz", xb.at[c, zl], xb.at[c, zl], zlp)

    recv(("tz", 0), tpiece(0, 1, x), zlp)
    t_to_x(0, 1)

    def w_left(p):
        recv(("wl", p), wpiece(3, s, p), zb)
        if p == 0:
            send(("wo", 0), wpiece(3, s, 0), wpiece(3, s, 0), zr)
        w_to_a(3, p)

    def w_right(p):
        recv(("wr", p), wpiece(1, s, p), zr)
        if p == 1:
            send(("wo", 1), wpiece(1, s, 1), wpiece(1, s, 1), zb)
        w_to_a(1, p)

    def t_from_x(slot, e):
        left, right = tpiece(slot, e, x_left), tpiece(slot, e, x_right)
        recv(("txl", slot, e), left, xl)
        if slot == 0:
            send(("txo", slot, e), left, left, xr)
        send(("ts", slot, e, 3), left, left, sib)
        recv(("txr", slot, e), right, xr)
        if slot == 1:
            send(("txo", slot, e), right, right, xl)
        send(("ts", slot, e, 1), right, right, sib)

    def t_from_opp(slot, e):
        opp = tpiece(slot, e, x_opp)
        recv(("txo", slot, e), opp, xl if slot == 0 else xr)
        send(("ts", slot, e, 2), opp, opp, sib)

    t_from_x(0, 0)
    w_left(0)
    w_right(1)
    recv(("tz", 1), tpiece(1, 1, x), zlp)
    t_to_x(1, 1)
    t_from_x(1, 0)
    recv("gz", xb.at[c, 1 - zl], zlp)
    send("gs", xb.at[c], xb.at[c], sib)
    t_from_x(0, 1)
    w_left(1)
    w_right(0)
    t_from_opp(0, 0)
    t_from_opp(1, 0)

    recv("gs", xb.at[1 - c], sib)
    my_cols = pl.ds(pl.multiple_of((zl * 2 + c) * kc, kc), kc)
    for a in range(2):
        lhs = xb[:, :, a, :, :, my_cols].reshape(n_tok, kc)
        rhs = xb[:, :, a].reshape(n_tok, BLOCK)
        gram = lax.dot_general(lhs, rhs, (((0,), (0,)), ((), ())), preferred_element_type=F32)
        for z in range(4):
            for q in range(4):
                gp[q, z, a] = gram[(z * 4 + q) * 16:(z * 4 + q + 1) * 16, :]
    for q in range(2):
        gbs[q] = gp[yy_of(1 - half, q)].astype(BF)

    t_from_x(1, 1)
    for p in range(2):
        recv(("wo", p), wpiece(2, s, p), zb if p == 0 else zr)
        w_to_a(2, p)
    t_from_opp(0, 1)
    t_from_opp(1, 1)

    for slot in range(2):
        for e in range(2):
            for r in range(4):
                recv(("ts", slot, e, r), tpiece(slot, e, (x + r) % 4, 1 - c), sib)
    for p in range(2):
        cols = pl.ds(p * n_tok // 2, n_tok // 2)
        recv(("h", p), ht.at[1, :, cols], yb)
    send("gb", gbs, gbr, yb)

    scale = 1.0 / math.sqrt(total)

    def down(r, q):
        cols = pl.ds(pl.multiple_of((zz(r) * 2 + q) * kc, kc), kc)
        acc = jnp.dot(ht[0], tok[0, :, :, :, :, cols].reshape(n_tok, kc), preferred_element_type=F32)
        acc += jnp.dot(ht[1], tok[1, :, :, :, :, cols].reshape(n_tok, kc), preferred_element_type=F32)
        return acc * scale

    def dpiece(ref, i, p):
        return ref.at[i, pl.ds(p * hf, hf), :]

    def down_to_a(r):
        asnd[r] = down(r, 1 - s).astype(BF)
        for p in (1, 0) if r == 1 else (0, 1):
            send(("da", r, p), dpiece(asnd, r, p), dpiece(arcv, r, p), ya)

    n_tile = n_tok // 4

    def hidden_grad(slot, i):
        lhs = tok[slot, i].reshape(n_tile, kc * 8)
        return jnp.dot(lhs, wf[...].reshape(kc * 8, ffl), preferred_element_type=F32)

    def hidden_to_b(i):
        at = pl.ds(i * n_tile, n_tile)
        snd[at, :] = hidden_grad(1, i).astype(BF)
        send(("gh", i), snd.at[at, :], rcv.at[at, :], yb)

    down_to_a(2)
    part[2] = down(2, s)
    for r in range(4):
        for p in range(2):
            recv(("wa", r, p), wpiece(r, 1 - s, p), ya)
    hidden_to_b(0)
    down_to_a(1)
    hidden_to_b(1)
    down_to_a(3)
    hidden_to_b(2)
    down_to_a(0)

    def reduced(r, p):
        recv(("da", r, p), dpiece(arcv, r, p), ya)
        at = pl.ds(p * hf, hf)
        return part[r, at, :] + arcv[r, at, :].astype(F32)

    zs[0] = reduced(2, 0).astype(BF)
    send(("z1", 0), zs.at[0], z1.at[0], zr)
    zs[1] = reduced(2, 1).astype(BF)
    send(("z1", 1), zs.at[1], z1.at[1], zb)
    hidden_to_b(3)
    part[1] = down(1, s)
    part[3] = down(3, s)

    recv("gb", gbr, yb)
    gas[...] = (gp[yy_of(half, 1 - s)] + gbr[1 - s].astype(F32)).astype(BF)
    send("ga", gas, gar, ya)
    gf[...] = gp[yy_of(half, s)] + gbr[s].astype(F32)

    zs[2] = reduced(1, 1).astype(BF)
    send(("z2r", 1), zs.at[2], dpiece(z2, 0, 1), zr)
    part[0] = down(0, s)
    zs[3] = reduced(3, 0).astype(BF)
    send(("z2l", 0), zs.at[3], dpiece(z2, 1, 0), zb)
    recv(("z1", 0), z1.at[0], zb)
    zs[4] = (reduced(1, 0) + z1[0].astype(F32)).astype(BF)
    send(("z2r", 0), zs.at[4], dpiece(z2, 0, 0), zr)
    recv(("z1", 1), z1.at[1], zr)
    zs[5] = (reduced(3, 1) + z1[1].astype(F32)).astype(BF)
    send(("z2l", 1), zs.at[5], dpiece(z2, 1, 1), zb)

    recv("ga", gar, ya)
    gf[...] += gar[...].astype(F32)
    gzs[0, 0] = gf[zz(2), 0].astype(BF)
    gzs[0, 1] = gf[zz(2), 1].astype(BF)
    send(("gz1", 0), gzs.at[0, 0], gz1.at[0], zr)
    send(("gz1", 1), gzs.at[0, 1], gz1.at[1], zb)

    for i in range(4):
        at = pl.ds(i * n_tile, n_tile)
        ghf[at, :] = hidden_grad(0, i)

    recv(("gz1", 0), gz1.at[0], zb)
    gzs[1, 0] = (gf[zz(1), 0] + gz1[0].astype(F32)).astype(BF)
    gzs[1, 1] = gf[zz(1), 1].astype(BF)
    send("gz2r", gzs.at[1], gz2.at[0], zr)
    recv(("gz1", 1), gz1.at[1], zr)
    gzs[2, 0] = gf[zz(3), 0].astype(BF)
    gzs[2, 1] = (gf[zz(3), 1] + gz1[1].astype(F32)).astype(BF)
    send("gz2l", gzs.at[2], gz2.at[1], zb)

    step = 32
    for i in range(4):
        at = pl.ds(i * n_tile, n_tile)
        recv(("gh", i), rcv.at[at, :], yb)

        @pl.loop(0, n_tile // step)
        def _(k):
            rows_at = pl.ds(pl.multiple_of(i * n_tile + k * step, step), step)
            gh = ghf[rows_at, :] + rcv[rows_at, :].astype(F32)
            gate = gate_ref[rows_at, :].astype(F32)
            up = up_ref[rows_at, :].astype(F32)
            sigma = jax.nn.sigmoid(gate)
            gu_ref[rows_at, :] = (gh * (gate * sigma)).astype(BF)
            gg_ref[rows_at, :] = (gh * up * sigma * (1.0 + gate * (1.0 - sigma))).astype(BF)

    recv("gz2r", gz2.at[0], zb)
    recv("gz2l", gz2.at[1], zr)
    for a, out in ((0, gi_ref), (1, go_ref)):
        out[...] = (gf[zh, a] + gz2[0, a].astype(F32) + gz2[1, a].astype(F32)) / total

    for p in range(2):
        at = pl.ds(p * hf, hf)
        recv(("z2r", p), dpiece(z2, 0, p), zb)
        recv(("z2l", p), dpiece(z2, 1, p), zr)
        own = reduced(0, p) + z2[0, at, :].astype(F32) + z2[1, at, :].astype(F32)
        gd_ref[at, :] = own.astype(BF)

    for cp in started:
        cp.wait_send()
    assert len(names) <= N_SEM, len(names)


N_SEM = 96


def shards(x_rows, grad_out, gate_pre, up_pre, down_weight):
    rows, width = x_rows.shape
    n_tok, ffl = gate_pre.shape
    kc = down_weight.shape[1]
    hf = ffl // 2
    total = float(rows * lax.axis_size("tensor") * lax.axis_size("dp"))
    gr = kc // 16
    vmem = pl.BlockSpec(memory_space=pltpu.VMEM)

    def kern(*refs):
        kernel(total, *refs)

    return pl.pallas_call(
        kern,
        out_shape=(
            jax.ShapeDtypeStruct((n_tok, ffl), BF),
            jax.ShapeDtypeStruct((n_tok, ffl), BF),
            jax.ShapeDtypeStruct((ffl, kc), BF),
            jax.ShapeDtypeStruct((gr, BLOCK), F32),
            jax.ShapeDtypeStruct((gr, BLOCK), F32),
        ),
        in_specs=[vmem] * 5,
        out_specs=(vmem,) * 5,
        scratch_shapes=[
            pltpu.VMEM((2, rows, width), BF),
            pltpu.VMEM((rows, kc * 8), BF),
            pltpu.VMEM((2, 4, 2, 2, rows, kc * 8), BF),
            pltpu.VMEM((8, kc, ffl), BF),
            pltpu.VMEM((2, ffl, n_tok), BF),
            pltpu.VMEM((2, 2, 2, 4, rows, BLOCK), BF),
            pltpu.VMEM((4, ffl, kc), BF),
            pltpu.VMEM((4, ffl, kc), BF),
            pltpu.VMEM((4, ffl, kc), F32),
            pltpu.VMEM((6, hf, kc), BF),
            pltpu.VMEM((2, hf, kc), BF),
            pltpu.VMEM((2, ffl, kc), BF),
            pltpu.VMEM((n_tok, ffl), BF),
            pltpu.VMEM((n_tok, ffl), BF),
            pltpu.VMEM((n_tok, ffl), F32),
            pltpu.VMEM((4, 4, 2, gr, BLOCK), F32),
            pltpu.VMEM((2, 4, 2, gr, BLOCK), BF),
            pltpu.VMEM((2, 4, 2, gr, BLOCK), BF),
            pltpu.VMEM((4, 2, gr, BLOCK), BF),
            pltpu.VMEM((4, 2, gr, BLOCK), BF),
            pltpu.VMEM((4, 2, gr, BLOCK), F32),
            pltpu.VMEM((3, 2, gr, BLOCK), BF),
            pltpu.VMEM((2, gr, BLOCK), BF),
            pltpu.VMEM((2, 2, gr, BLOCK), BF),
            pltpu.SemaphoreType.DMA((N_SEM,)),
            pltpu.SemaphoreType.DMA((N_SEM,)),
        ],
        compiler_params=pltpu.CompilerParams(
            collective_id=0, has_side_effects=True, vmem_limit_bytes=60 * 1024 * 1024
        ),
        cost_estimate=pl.CostEstimate(
            flops=4 * n_tok * width * ffl, bytes_accessed=8 * n_tok * ffl, transcendentals=0
        ),
    )(x_rows, grad_out, gate_pre, up_pre, down_weight)


def solution(mesh):
    return jax.shard_map(
        shards,
        mesh=mesh,
        in_specs=(
            P(("dp", "tensor"), None),
            P(("dp", "tensor"), None),
            P("dp", "tensor"),
            P("dp", "tensor"),
            P("tensor", "dp"),
        ),
        out_specs=(
            P("dp", "tensor"),
            P("dp", "tensor"),
            P("tensor", "dp"),
            P(("tensor", "dp"), None),
            P(("tensor", "dp"), None),
        ),
        check_vma=False,
    )
```

time: 599 us -> 148 us (0.25)
  waiting for transfers between devices: 551 us -> 0 us
  Pallas kernels: 0 us -> 141 us
  matrix products: 30.3 us -> 0 us
  between operations: 13.8 us -> 0.66 us
    all_gather x3 -> x0, waiting for transfers between devices: 197 us -> none  [the longest x1 103 us: shards(): lax.all_gather(down_weight, 'dp', axis=1, tiled=True)]
    reduce_scatter x1 -> x0, waiting for transfers between devices: 192 us -> none  [shards(): lax.psum_scatter(partial_grad, 'dp', scatter_dimension=1, tiled=True)]
    psum x1 -> x0, waiting for transfers between devices: 160 us -> none  [shards(): gram_in_all, gram_out_all = lax.psum((gram_in_part, gram_out_part), 'dp')]
    pallas_call x0 -> x1, Pallas kernels: none -> 141 us  [shards(): pl.pallas_call(kern, out_shape=(jax.ShapeDtypeStruct((n_tok, ffl), BF), j...]
    dot_general x4 -> x0, matrix products: 30.3 us -> none  [the longest x1 12.7 us: shards(): lax.dot_general(grad_rows, lax.all_gather(down_weight, 'dp', axis=1, tile...]
  transfers between devices with their start and end apart: 5 -> 0, of which waited for: 5 -> 0; matrix products, arithmetic and copies ran while one was open for 5% -> 0% of each run, Pallas kernels for 0% -> 0%
where the time goes in v1:
time: 148 us; the launch traced here: 147 us
  Pallas kernels  141 us (95%)
  local copies, waits for them, and re-layouts  5.94 us (4%)
    pallas_call x1, Pallas kernels, shards(): pl.pallas_call(kern, out_shape=(jax.ShapeDtypeStruct((n_tok, ffl), BF), j...  141 us
    unnamed x13, local copies, waits for them, and re-layouts  5.94 us

profile of v1, /device:TPU:1, one launch (start us, length us, event | category | flops | bytes accessed | tf_op | source)
XLA Modules:
  0.0 147.2 jit_solution(18059388334988009518)
XLA Ops:
  0.6 140.6 %shard_map.92 = (bf16[768,896]{1,0:T(8,128)(2,1)}, bf16[768,896]{1,0:T(8,128)(2,1)}, bf16[896,256]{1,0:T(8,128)(2,1)}, f32[16,1024]{1,0:T(8,128)}, f32[16,1024]{1,0:T(8,128)}) custom-call(bf16[48,4096]{1,0:T(8,128)(2,1)} %refs_0_.1, bf16[48,4096]{1,0:T(8,128)(2,1)} %refs_1_.1, bf16[768,896]{1,0:T(8,128)(2,1)} %refs_2_.1, bf16[768,896]{1,0:T(8,128)(2,1)} %refs_3_.1, ...), custom_call_target="tpu_custom_call" | custom-call | flops 11274289152 | bytes 5505024 | tf_op jit(solution)/shard_map/pallas_call | solution.py:359
  141.2 0.0 copy-start
  141.3 2.6 %copy.15 = bf16[768,896]{1,0:T(8,128)(2,1)} copy(bf16[768,896]{1,0:T(8,128)(2,1)} %get-tuple-element.10) | data formatting | bytes 2752512
  143.9 0.0 copy-done
  143.9 0.0 copy-start.1
  143.9 0.0 copy-start.3
  143.9 0.0 copy-start.2
  143.9 1.1 copy.16
  145.0 0.2 copy-done.1
  145.2 0.8 copy.17
  145.9 0.0 copy-done.3
  145.9 0.6 copy.18
  146.6 0.0 copy-done.2
  146.6 0.6 copy.19
Async XLA Ops:
  141.2 2.6 %copy-start = (bf16[768,896]{1,0:T(8,128)(2,1)S(1)}, bf16[768,896]{1,0:T(8,128)(2,1)}, u32[]{:S(2)}) copy-start(bf16[768,896]{1,0:T(8,128)(2,1)} %get-tuple-element.11) | copy-start | bytes 4128772
  143.9 1.3 copy-start.1
  143.9 2.0 %copy-start.3 = (f32[16,1024]{1,0:T(8,128)S(1)}, f32[16,1024]{1,0:T(8,128)}, u32[]{:S(2)}) copy-start(f32[16,1024]{1,0:T(8,128)} %get-tuple-element.13) | copy-start | bytes 196612
  143.9 2.7 %copy-start.2 = (f32[16,1024]{1,0:T(8,128)S(1)}, f32[16,1024]{1,0:T(8,128)}, u32[]{:S(2)}) copy-start(f32[16,1024]{1,0:T(8,128)} %get-tuple-element.14) | copy-start | bytes 196612

commit v2 on v1

v2 whole, which is shorter than its diff:
```python
import math

import jax
import jax.numpy as jnp
from jax import lax
from jax.experimental import pallas as pl
from jax.experimental.pallas import tpu as pltpu
from jax.sharding import PartitionSpec as P

MESH = pl.DeviceIdType.MESH
BF = jnp.bfloat16
F32 = jnp.float32
BLOCK = 1024
N_SEM = 128
SPLIT = 512


def kernel(
    total,
    x_hbm, g_hbm, gate_hbm, up_hbm, w_hbm,
    gg_hbm, gu_hbm, gd_hbm, gi_hbm, go_hbm,
    x_ref, g_ref, gate_ref, up_ref, w_ref,
    gg_ref, gu_ref, gd_ref, gi_ref, go_ref,
    ghalf, tok, wf0, wf1, ht, xi, xo_buf, gm, asnd, arcv, part, zs, z1, z2,
    snd0, snd1, rcv0, rcv1, ghf, gp, gbs, gbr, gas, gar, gf, gzs, gz1, gz2,
    ssem, rsem, isem, osem,
):
    rows = g_ref.shape[0]
    ffl, kc = w_ref.shape
    n_tok = gate_ref.shape[0]
    hk = kc // 2
    hf = ffl // 2
    hcols = (pl.ds(0, SPLIT), pl.ds(SPLIT, ffl - SPLIT))
    d = lax.axis_index("dp")
    t = lax.axis_index("tensor")
    zh, y = d // 4, d % 4
    x, zl, c = t // 4, (t // 2) % 2, t % 2
    half = ((y + 1) // 2) % 2
    s = y // 2

    sib = (d, t + 1 - 2 * c)
    zlp = (d, t + 2 - 4 * zl)
    xr = (d, ((x + 1) % 4) * 4 + t % 4)
    xl = (d, ((x + 3) % 4) * 4 + t % 4)
    xo = (d, ((x + 2) % 4) * 4 + t % 4)
    ya = (zh * 4 + 3 - y, t)
    yb = (zh * 4 + y + 1 - 2 * (y % 2), t)
    zr = (((zh + 1) % 4) * 4 + y, t)
    zb = (((zh + 3) % 4) * 4 + y, t)
    zo = (((zh + 3 + 2 * zl) % 4) * 4 + y, t + 2 - 4 * zl)
    neighbours = (sib, zlp, zo, xr, xl, xo, ya, yb, zr, zb)

    barrier = pltpu.get_barrier_semaphore()
    for n in neighbours:
        pl.semaphore_signal(barrier, inc=1, device_id=n, device_id_type=MESH)
    loads = [
        pltpu.make_async_copy(a, b, isem.at[i])
        for i, (a, b) in enumerate(
            ((w_hbm, w_ref), (g_hbm, g_ref), (gate_hbm, gate_ref), (up_hbm, up_ref), (x_hbm, x_ref))
        )
    ]
    for cp in loads:
        cp.start()

    names = {}
    started = []
    stores = []

    def sem(key):
        return names.setdefault(key, len(names))

    def send(key, src_ref, dst_ref, dev):
        k = sem(key)
        cp = pltpu.make_async_remote_copy(
            src_ref=src_ref, dst_ref=dst_ref, send_sem=ssem.at[k], recv_sem=rsem.at[k],
            device_id=dev, device_id_type=MESH,
        )
        cp.start()
        started.append(cp)

    def recv(key, dst_ref, dev):
        k = sem(key)
        pltpu.make_async_remote_copy(
            src_ref=dst_ref, dst_ref=dst_ref, send_sem=ssem.at[k], recv_sem=rsem.at[k],
            device_id=dev, device_id_type=MESH,
        ).wait_recv()

    def store(src_ref, dst_ref):
        cp = pltpu.make_async_copy(src_ref, dst_ref, osem.at[len(stores)])
        cp.start()
        stores.append(cp)

    def zz(r):
        return (zh + r) % 4

    def yy_of(h, q):
        return h + q * (3 - 2 * h)

    def wpiece(r, q, hh, kh=None):
        ref = (wf0, wf1)[hh]
        if kh is None:
            return ref.at[zz(r) * 2 + q]
        return ref.at[zz(r) * 2 + q, pl.ds(kh * hk, hk), :]

    def w_to_a(r, hh, kh=None):
        send(("wa", r, hh, kh), wpiece(r, s, hh, kh), wpiece(r, s, hh, kh), ya)

    def w_own(hh, i):
        send(("wl", hh, i), wpiece(0, s, hh, i), wpiece(0, s, hh, i), zr)
        send(("wr", hh, i), wpiece(0, s, hh, 1 - i), wpiece(0, s, hh, 1 - i), zb)

    def w_mid(hh, i):
        recv(("wl", hh, i), wpiece(3, s, hh, i), zb)
        if i == 0:
            send(("wo", hh, 0), wpiece(3, s, hh, 0), wpiece(3, s, hh, 0), zr)
        recv(("wr", hh, i), wpiece(1, s, hh, 1 - i), zr)
        if i == 0:
            send(("wo", hh, 1), wpiece(1, s, hh, 1), wpiece(1, s, hh, 1), zb)
        w_to_a(3, hh, i)
        w_to_a(1, hh, 1 - i)

    def w_opp(hh, kh):
        recv(("wo", hh, kh), wpiece(2, s, hh, kh), zb if kh == 0 else zr)
        w_to_a(2, hh, kh)

    def w_from_a(hh):
        recv(("wa", 0, hh, None), wpiece(0, 1 - s, hh), ya)
        for r in (3, 1, 2):
            for kh in range(2):
                recv(("wa", r, hh, kh), wpiece(r, 1 - s, hh, kh), ya)

    loads[0].wait()
    wf0[zh * 2 + s] = w_ref[:SPLIT, :].astype(F32).T.astype(BF)
    wf1[zh * 2 + s] = w_ref[SPLIT:, :].astype(F32).T.astype(BF)

    loads[1].wait()
    for z in range(4):
        for q in range(2):
            to = pl.ds((z * 2 + q) * kc, kc)
            other = pl.multiple_of((z * 4 + yy_of(1 - half, q)) * kc, kc)
            mine = pl.multiple_of((z * 4 + yy_of(half, q)) * kc, kc)
            ghalf[:, to] = g_ref[:, pl.ds(other, kc)]
            tok[0, x, zl, c, :, to] = g_ref[:, pl.ds(mine, kc)]

    pl.semaphore_wait(barrier, len(neighbours))

    w_to_a(0, 0)
    w_own(0, 0)
    w_own(0, 1)

    def tpiece(slot, e, xx, cc=c):
        return tok.at[slot, xx, zl if e == 0 else 1 - zl, cc]

    x_left, x_right, x_opp = (x + 3) % 4, (x + 1) % 4, (x + 2) % 4

    def t_to_x(slot, e):
        ref = tpiece(slot, e, x)
        send(("txl", slot, e), ref, ref, xr)
        send(("txr", slot, e), ref, ref, xl)
        send(("ts", slot, e, 0), ref, ref, sib)

    def t_from_x(slot, e):
        left, right = tpiece(slot, e, x_left), tpiece(slot, e, x_right)
        recv(("txl", slot, e), left, xl)
        if slot == 0:
            send(("txo", slot, e), left, left, xr)
        send(("ts", slot, e, 3), left, left, sib)
        recv(("txr", slot, e), right, xr)
        if slot == 1:
            send(("txo", slot, e), right, right, xl)
        send(("ts", slot, e, 1), right, right, sib)

    def t_from_opp(slot, e):
        opp = tpiece(slot, e, x_opp)
        recv(("txo", slot, e), opp, xl if slot == 0 else xr)
        send(("ts", slot, e, 2), opp, opp, sib)

    def t_to_z(slot):
        send(("tz", slot), tpiece(slot, 0, x), tpiece(slot, 0, x), zlp)

    send("tb", ghalf, tok.at[1, x, zl, c], yb)
    t_to_x(0, 0)
    w_to_a(0, 1)

    loads[2].wait()
    loads[3].wait()
    ht_tile = 128

    def hidden_tile(i):
        at = pl.ds(pl.multiple_of(i * ht_tile, ht_tile), ht_tile)
        gate = gate_ref[at, :].astype(F32)
        up = up_ref[at, :].astype(F32)
        hid = (gate * jax.nn.sigmoid(gate) * up).astype(BF)
        ht[0, :, at] = hid.astype(F32).T.astype(BF)

    n_ht = n_tok // ht_tile
    for p in range(2):
        pl.loop(p * n_ht // 2, (p + 1) * n_ht // 2)(hidden_tile)
        cols = pl.ds(p * n_tok // 2, n_tok // 2)
        send(("h", p), ht.at[0, :, cols], ht.at[1, :, cols], yb)

    loads[4].wait()

    def x_cols(xx):
        return pl.ds(pl.multiple_of(xx * BLOCK, BLOCK), BLOCK)

    def o_cols(xx):
        return pl.ds(pl.multiple_of(xx * 2 * kc, 2 * kc), 2 * kc)

    xi[c, zl, x] = x_ref[:, x_cols(x)]
    xo_buf[c, zl, x] = ghalf[:, o_cols(x)]
    for r, dev in ((1, xr), (3, xl), (2, xo)):
        send(("gxi", r), x_ref.at[:, x_cols((x + r) % 4)], xi.at[c, zl, x], dev)

    recv("tb", tpiece(1, 0, x), yb)
    t_to_x(1, 0)
    w_mid(0, 0)
    t_from_x(0, 0)
    w_mid(0, 1)
    t_to_z(0)
    t_to_z(1)
    for r, dev in ((3, xr), (1, xl), (2, xo)):
        recv(("gxi", r), xi.at[c, zl, (x + 4 - r) % 4], dev)
    send("gzi", xi.at[c, zl], xi.at[c, zl], zo)
    t_from_x(1, 0)
    w_opp(0, 0)
    w_opp(0, 1)
    w_own(1, 0)
    recv(("tz", 0), tpiece(0, 1, x), zlp)
    t_to_x(0, 1)
    recv(("tz", 1), tpiece(1, 1, x), zlp)
    t_to_x(1, 1)
    w_own(1, 1)
    t_from_x(0, 1)
    recv("gzi", xi.at[c, 1 - zl], zo)
    send("gsi", xi.at[c], xi.at[c], sib)
    w_mid(1, 0)
    t_from_x(1, 1)
    for r, dev in ((1, xr), (3, xl), (2, xo)):
        send(("gxo", r), ghalf.at[:, o_cols((x + r) % 4)], xo_buf.at[c, zl, x], dev)

    recv("gsi", xi.at[1 - c], sib)
    my_cols = pl.ds(pl.multiple_of((zl * 2 + c) * kc, kc), kc)

    def gram(a, ref):
        lhs, rhs = ref[:, :, :, :, my_cols].reshape(n_tok, kc), ref[...].reshape(n_tok, BLOCK)
        out = lax.dot_general(lhs, rhs, (((0,), (0,)), ((), ())), preferred_element_type=F32)
        for z in range(4):
            for q in range(4):
                gp[a, q, z] = out[(z * 4 + q) * 16:(z * 4 + q + 1) * 16, :]
        for q in range(2):
            gbs[a, q] = gp[a, yy_of(1 - half, q)].astype(BF)

    gram(0, xi)
    w_mid(1, 1)
    t_from_opp(0, 0)
    t_from_opp(1, 0)
    t_from_opp(0, 1)
    t_from_opp(1, 1)
    w_opp(1, 0)
    w_opp(1, 1)
    for r, dev in ((3, xr), (1, xl), (2, xo)):
        recv(("gxo", r), xo_buf.at[c, zl, (x + 4 - r) % 4], dev)
    send("gzo", xo_buf.at[c, zl], xo_buf.at[c, zl], zlp)
    for p in range(2):
        cols = pl.ds(p * n_tok // 2, n_tok // 2)
        recv(("h", p), ht.at[1, :, cols], yb)
    send(("gb", 0), gbs.at[0], gbr.at[0], yb)

    for slot in range(2):
        for e in range(2):
            for r in range(4):
                recv(("ts", slot, e, r), tpiece(slot, e, (x + r) % 4, 1 - c), sib)

    scale = 1.0 / math.sqrt(total)

    def down(r, q):
        cols = pl.ds(pl.multiple_of((zz(r) * 2 + q) * kc, kc), kc)
        acc = jnp.dot(ht[0], tok[0, :, :, :, :, cols].reshape(n_tok, kc), preferred_element_type=F32)
        acc += jnp.dot(ht[1], tok[1, :, :, :, :, cols].reshape(n_tok, kc), preferred_element_type=F32)
        return acc * scale

    def dpiece(ref, i, p):
        return ref.at[i, pl.ds(p * hf, hf), :]

    def down_to_a(r, p):
        send(("da", r, p), dpiece(asnd, r, p), dpiece(arcv, r, p), ya)

    n_tile = n_tok // 2

    def hidden_grad(slot, hh, i):
        lhs = tok[slot, 2 * i:2 * i + 2].reshape(n_tile, kc * 8)
        rhs = wf0[...].reshape(kc * 8, SPLIT) if hh == 0 else wf1[...].reshape(kc * 8, ffl - SPLIT)
        return jnp.dot(lhs, rhs, preferred_element_type=F32)

    def hidden_to_b(hh, i):
        at = pl.ds(i * n_tile, n_tile)
        snd, rcv = (snd0, snd1)[hh], (rcv0, rcv1)[hh]
        send(("gh", hh, i), snd.at[at, :], rcv.at[at, :], yb)

    w_from_a(0)
    for i in range(2):
        snd0[i * n_tile:(i + 1) * n_tile, :] = hidden_grad(1, 0, i).astype(BF)
        hidden_to_b(0, i)
    asnd[2] = down(2, 1 - s).astype(BF)
    down_to_a(2, 0)
    down_to_a(2, 1)
    asnd[1] = down(1, 1 - s).astype(BF)
    asnd[3] = down(3, 1 - s).astype(BF)
    part[2] = down(2, s)
    w_from_a(1)
    for i in range(2):
        snd1[i * n_tile:(i + 1) * n_tile, :] = hidden_grad(1, 1, i).astype(BF)

    def reduced(r, p):
        recv(("da", r, p), dpiece(arcv, r, p), ya)
        at = pl.ds(p * hf, hf)
        return part[r, at, :] + arcv[r, at, :].astype(F32)

    def gram_to_a(a):
        recv(("gb", a), gbr.at[a], yb)
        gas[a] = (gp[a, yy_of(half, 1 - s)] + gbr[a, 1 - s].astype(F32)).astype(BF)
        send(("ga", a), gas.at[a], gar.at[a], ya)
        gf[a] = gp[a, yy_of(half, s)] + gbr[a, s].astype(F32)

    def gram_z1(a):
        recv(("ga", a), gar.at[a], ya)
        gf[a] = gf[a] + gar[a].astype(F32)
        gzs[a, 0] = gf[a, zz(2)].astype(BF)
        send(("gz1", a), gzs.at[a, 0], gz1.at[a], zr if a == 0 else zb)

    def gram_z2(a):
        recv(("gz1", a), gz1.at[a], zb if a == 0 else zr)
        passed = gz1[a].astype(F32)
        gzs[a, 1] = (gf[a, zz(1)] + passed if a == 0 else gf[a, zz(1)]).astype(BF)
        send(("gz2r", a), gzs.at[a, 1], gz2.at[a, 0], zr)
        gzs[a, 2] = (gf[a, zz(3)] + passed if a == 1 else gf[a, zz(3)]).astype(BF)
        send(("gz2l", a), gzs.at[a, 2], gz2.at[a, 1], zb)

    def gram_out(a, out, hbm):
        recv(("gz2r", a), gz2.at[a, 0], zb)
        recv(("gz2l", a), gz2.at[a, 1], zr)
        out[...] = (gf[a, zh] + gz2[a, 0].astype(F32) + gz2[a, 1].astype(F32)) / total
        store(out, hbm)

    gram_to_a(0)
    recv("gzo", xo_buf.at[c, 1 - zl], zlp)
    send("gso", xo_buf.at[c], xo_buf.at[c], sib)
    for q in range(2):
        mine = pl.ds(pl.multiple_of(yy_of(half, q) * kc, kc), kc)
        from_tok = pl.ds(pl.multiple_of((x * 2 + q) * kc, kc), kc)
        for cc in range(2):
            for zc in range(2):
                for xc in range(4):
                    gm[cc, zc, xc, :, mine] = tok[0, xc, zc, cc, :, from_tok]
    recv("gso", xo_buf.at[1 - c], sib)
    for q in range(2):
        other = pl.ds(pl.multiple_of(yy_of(1 - half, q) * kc, kc), kc)
        gm[:, :, :, :, other] = xo_buf[:, :, :, :, q * kc:(q + 1) * kc]
    gram(1, gm)
    send(("gb", 1), gbs.at[1], gbr.at[1], yb)
    hidden_to_b(1, 0)
    hidden_to_b(1, 1)

    zs[0] = reduced(2, 0).astype(BF)
    send(("z1", 0), zs.at[0], z1.at[0], zr)
    down_to_a(1, 1)
    down_to_a(3, 0)
    zs[1] = reduced(2, 1).astype(BF)
    send(("z1", 1), zs.at[1], z1.at[1], zb)
    down_to_a(1, 0)
    down_to_a(3, 1)
    gram_z1(0)
    part[1] = down(1, s)
    part[3] = down(3, s)
    asnd[0] = down(0, 1 - s).astype(BF)
    gram_z2(0)
    gram_to_a(1)
    zs[2] = reduced(1, 1).astype(BF)
    send(("z2r", 1), zs.at[2], dpiece(z2, 0, 1), zr)
    zs[3] = reduced(3, 0).astype(BF)
    send(("z2l", 0), zs.at[3], dpiece(z2, 1, 0), zb)
    down_to_a(0, 0)
    down_to_a(0, 1)
    gram_z1(1)

    recv(("z1", 0), z1.at[0], zb)
    zs[4] = (reduced(1, 0) + z1[0].astype(F32)).astype(BF)
    send(("z2r", 0), zs.at[4], dpiece(z2, 0, 0), zr)
    recv(("z1", 1), z1.at[1], zr)
    zs[5] = (reduced(3, 1) + z1[1].astype(F32)).astype(BF)
    send(("z2l", 1), zs.at[5], dpiece(z2, 1, 1), zb)

    part[0] = down(0, s)
    for hh in range(2):
        for i in range(2):
            ghf[i * n_tile:(i + 1) * n_tile, hcols[hh]] = hidden_grad(0, hh, i)

    step = 32

    def finish(hh):
        rcv, cols = (rcv0, rcv1)[hh], hcols[hh]
        for i in range(2):
            at = pl.ds(i * n_tile, n_tile)
            recv(("gh", hh, i), rcv.at[at, :], yb)

            @pl.loop(0, n_tile // step)
            def _(k):
                rows_at = pl.ds(pl.multiple_of(i * n_tile + k * step, step), step)
                gh = ghf[rows_at, cols] + rcv[rows_at, :].astype(F32)
                gate = gate_ref[rows_at, cols].astype(F32)
                up = up_ref[rows_at, cols].astype(F32)
                sigma = jax.nn.sigmoid(gate)
                gu_ref[rows_at, cols] = (gh * (gate * sigma)).astype(BF)
                gg_ref[rows_at, cols] = (gh * up * sigma * (1.0 + gate * (1.0 - sigma))).astype(BF)

            store(gu_ref.at[at, cols], gu_hbm.at[at, cols])
            store(gg_ref.at[at, cols], gg_hbm.at[at, cols])

    finish(0)

    gram_z2(1)
    gram_out(0, gi_ref, gi_hbm)
    finish(1)
    gram_out(1, go_ref, go_hbm)

    for p in range(2):
        at = pl.ds(p * hf, hf)
        recv(("z2r", p), dpiece(z2, 0, p), zb)
        recv(("z2l", p), dpiece(z2, 1, p), zr)
        own = reduced(0, p) + z2[0, at, :].astype(F32) + z2[1, at, :].astype(F32)
        gd_ref[at, :] = own.astype(BF)
        store(gd_ref.at[at, :], gd_hbm.at[at, :])

    for cp in started:
        cp.wait_send()
    for cp in stores:
        cp.wait()
    assert len(names) <= N_SEM and len(stores) <= 16, (len(names), len(stores))


def shards(x_rows, grad_out, gate_pre, up_pre, down_weight):
    rows, width = x_rows.shape
    n_tok, ffl = gate_pre.shape
    kc = down_weight.shape[1]
    hf = ffl // 2
    total = float(rows * lax.axis_size("tensor") * lax.axis_size("dp"))
    gr = kc // 16
    hbm = pl.BlockSpec(memory_space=pl.ANY)

    def kern(*refs):
        kernel(total, *refs)

    outs = [
        ((n_tok, ffl), BF),
        ((n_tok, ffl), BF),
        ((ffl, kc), BF),
        ((gr, BLOCK), F32),
        ((gr, BLOCK), F32),
    ]
    return pl.pallas_call(
        kern,
        out_shape=tuple(jax.ShapeDtypeStruct(*o) for o in outs),
        in_specs=[hbm] * 5,
        out_specs=(hbm,) * 5,
        scratch_shapes=[
            pltpu.VMEM((rows, width), BF),
            pltpu.VMEM((rows, width), BF),
            pltpu.VMEM((n_tok, ffl), BF),
            pltpu.VMEM((n_tok, ffl), BF),
            pltpu.VMEM((ffl, kc), BF),
            *(pltpu.VMEM(*o) for o in outs),
            pltpu.VMEM((rows, kc * 8), BF),
            pltpu.VMEM((2, 4, 2, 2, rows, kc * 8), BF),
            pltpu.VMEM((8, kc, SPLIT), BF),
            pltpu.VMEM((8, kc, ffl - SPLIT), BF),
            pltpu.VMEM((2, ffl, n_tok), BF),
            pltpu.VMEM((2, 2, 4, rows, BLOCK), BF),
            pltpu.VMEM((2, 2, 4, rows, 2 * kc), BF),
            pltpu.VMEM((2, 2, 4, rows, BLOCK), BF),
            pltpu.VMEM((4, ffl, kc), BF),
            pltpu.VMEM((4, ffl, kc), BF),
            pltpu.VMEM((4, ffl, kc), F32),
            pltpu.VMEM((6, hf, kc), BF),
            pltpu.VMEM((2, hf, kc), BF),
            pltpu.VMEM((2, ffl, kc), BF),
            pltpu.VMEM((n_tok, SPLIT), BF),
            pltpu.VMEM((n_tok, ffl - SPLIT), BF),
            pltpu.VMEM((n_tok, SPLIT), BF),
            pltpu.VMEM((n_tok, ffl - SPLIT), BF),
            pltpu.VMEM((n_tok, ffl), F32),
            pltpu.VMEM((2, 4, 4, gr, BLOCK), F32),
            pltpu.VMEM((2, 2, 4, gr, BLOCK), BF),
            pltpu.VMEM((2, 2, 4, gr, BLOCK), BF),
            pltpu.VMEM((2, 4, gr, BLOCK), BF),
            pltpu.VMEM((2, 4, gr, BLOCK), BF),
            pltpu.VMEM((2, 4, gr, BLOCK), F32),
            pltpu.VMEM((2, 3, gr, BLOCK), BF),
            pltpu.VMEM((2, gr, BLOCK), BF),
            pltpu.VMEM((2, 2, gr, BLOCK), BF),
            pltpu.SemaphoreType.DMA((N_SEM,)),
            pltpu.SemaphoreType.DMA((N_SEM,)),
            pltpu.SemaphoreType.DMA((5,)),
            pltpu.SemaphoreType.DMA((16,)),
        ],
        compiler_params=pltpu.CompilerParams(
            collective_id=0, has_side_effects=True, vmem_limit_bytes=60 * 1024 * 1024
        ),
        cost_estimate=pl.CostEstimate(
            flops=4 * n_tok * width * ffl, bytes_accessed=8 * n_tok * ffl, transcendentals=0
        ),
    )(x_rows, grad_out, gate_pre, up_pre, down_weight)


def solution(mesh):
    return jax.shard_map(
        shards,
        mesh=mesh,
        in_specs=(
            P(("dp", "tensor"), None),
            P(("dp", "tensor"), None),
            P("dp", "tensor"),
            P("dp", "tensor"),
            P("tensor", "dp"),
        ),
        out_specs=(
            P("dp", "tensor"),
            P("dp", "tensor"),
            P("tensor", "dp"),
            P(("tensor", "dp"), None),
            P(("tensor", "dp"), None),
        ),
        check_vma=False,
    )
```

time: 148 us -> 117 us (0.79)
  Pallas kernels: 141 us -> 110 us
    pallas_call x1, Pallas kernels: 141 us -> 110 us  [shards(): pl.pallas_call(kern, out_shape=tuple((jax.ShapeDtypeStruct(*o) for o in o...]
where the time goes in v2:
time: 117 us
  Pallas kernels  110 us (94%)
  local copies, waits for them, and re-layouts  5.94 us (5%)
    pallas_call x1, Pallas kernels, shards(): pl.pallas_call(kern, out_shape=tuple((jax.ShapeDtypeStruct(*o) for o in o...  110 us
    unnamed x13, local copies, waits for them, and re-layouts  5.94 us

profile of v2, /device:TPU:1, one launch (start us, length us, event | category | flops | bytes accessed | tf_op | source)
XLA Modules:
  0.0 116.5 jit_solution(18042248881852705024)
XLA Ops:
  0.6 109.9 %shard_map.92 = (bf16[768,896]{1,0:T(8,128)(2,1)}, bf16[768,896]{1,0:T(8,128)(2,1)}, bf16[896,256]{1,0:T(8,128)(2,1)}, f32[16,1024]{1,0:T(8,128)}, f32[16,1024]{1,0:T(8,128)}) custom-call(bf16[48,4096]{1,0:T(8,128)(2,1)} %refs_0_.1, bf16[48,4096]{1,0:T(8,128)(2,1)} %refs_1_.1, bf16[768,896]{1,0:T(8,128)(2,1)} %refs_2_.1, bf16[768,896]{1,0:T(8,128)(2,1)} %refs_3_.1, ...), custom_call_target="tpu_custom_call" | custom-call | flops 11274289152 | bytes 5505024 | tf_op jit(solution)/shard_map/pallas_call | solution.py:461
  110.6 0.0 copy-start
  110.6 2.6 %copy.15 = bf16[768,896]{1,0:T(8,128)(2,1)} copy(bf16[768,896]{1,0:T(8,128)(2,1)} %get-tuple-element.10) | data formatting | bytes 2752512
  113.2 0.0 copy-done
  113.2 0.0 copy-start.1
  113.2 0.0 copy-start.3
  113.2 0.0 copy-start.2
  113.2 1.1 copy.16
  114.3 0.2 copy-done.1
  114.5 0.8 copy.17
  115.3 0.0 copy-done.3
  115.3 0.6 copy.18
  115.9 0.0 copy-done.2
  115.9 0.6 copy.19
Async XLA Ops:
  110.6 2.6 %copy-start = (bf16[768,896]{1,0:T(8,128)(2,1)S(1)}, bf16[768,896]{1,0:T(8,128)(2,1)}, u32[]{:S(2)}) copy-start(bf16[768,896]{1,0:T(8,128)(2,1)} %get-tuple-element.11) | copy-start | bytes 4128772
  113.2 1.3 %copy-start.1 = (bf16[896,256]{1,0:T(8,128)(2,1)S(1)}, bf16[896,256]{1,0:T(8,128)(2,1)}, u32[]{:S(2)}) copy-start(bf16[896,256]{1,0:T(8,128)(2,1)} %get-tuple-element.12) | copy-start | bytes 1376260
  113.2 2.0 %copy-start.3 = (f32[16,1024]{1,0:T(8,128)S(1)}, f32[16,1024]{1,0:T(8,128)}, u32[]{:S(2)}) copy-start(f32[16,1024]{1,0:T(8,128)} %get-tuple-element.13) | copy-start | bytes 196612
  113.2 2.7 %copy-start.2 = (f32[16,1024]{1,0:T(8,128)S(1)}, f32[16,1024]{1,0:T(8,128)}, u32[]{:S(2)}) copy-start(f32[16,1024]{1,0:T(8,128)} %get-tuple-element.14) | copy-start | bytes 196612

commit v3 on v2

--- a/solution.py
+++ b/solution.py
@@ -13,6 +13,7 @@
 BLOCK = 1024
 N_SEM = 128
 SPLIT = 512
+FIRST = 128
 
 
 def kernel(
@@ -22,6 +23,7 @@
     x_ref, g_ref, gate_ref, up_ref, w_ref,
     gg_ref, gu_ref, gd_ref, gi_ref, go_ref,
     ghalf, tok, wf0, wf1, ht, xi, xo_buf, gm, asnd, arcv, part, zs, z1, z2,
+    fp, fs1, fs2, f1, f2, fas, far,
     snd0, snd1, rcv0, rcv1, ghf, gp, gbs, gbr, gas, gar, gf, gzs, gz1, gz2,
     ssem, rsem, isem, osem,
 ):
@@ -29,7 +31,8 @@
     ffl, kc = w_ref.shape
     n_tok = gate_ref.shape[0]
     hk = kc // 2
-    hf = ffl // 2
+    hd = ffl - FIRST
+    hf = hd // 2
     hcols = (pl.ds(0, SPLIT), pl.ds(SPLIT, ffl - SPLIT))
     d = lax.axis_index("dp")
     t = lax.axis_index("tensor")
@@ -159,20 +162,24 @@
         send(("txr", slot, e), ref, ref, xl)
         send(("ts", slot, e, 0), ref, ref, sib)
 
+    wide = kc * 4
+
+    def thalf(ref, p):
+        return ref.at[:, pl.ds(p * wide, wide)]
+
     def t_from_x(slot, e):
         left, right = tpiece(slot, e, x_left), tpiece(slot, e, x_right)
         recv(("txl", slot, e), left, xl)
-        if slot == 0:
-            send(("txo", slot, e), left, left, xr)
+        send(("txo", slot, e, 0), thalf(left, 0), thalf(left, 0), xr)
         send(("ts", slot, e, 3), left, left, sib)
         recv(("txr", slot, e), right, xr)
-        if slot == 1:
-            send(("txo", slot, e), right, right, xl)
+        send(("txo", slot, e, 1), thalf(right, 1), thalf(right, 1), xl)
         send(("ts", slot, e, 1), right, right, sib)
 
     def t_from_opp(slot, e):
         opp = tpiece(slot, e, x_opp)
-        recv(("txo", slot, e), opp, xl if slot == 0 else xr)
+        recv(("txo", slot, e, 0), thalf(opp, 0), xl)
+        recv(("txo", slot, e, 1), thalf(opp, 1), xr)
         send(("ts", slot, e, 2), opp, opp, sib)
 
     def t_to_z(slot):
@@ -211,6 +218,20 @@
     xo_buf[c, zl, x] = ghalf[:, o_cols(x)]
     for r, dev in ((1, xr), (3, xl), (2, xo)):
         send(("gxi", r), x_ref.at[:, x_cols((x + r) % 4)], xi.at[c, zl, x], dev)
+        send(("gxo", r), ghalf.at[:, o_cols((x + r) % 4)], xo_buf.at[c, zl, x], dev)
+
+    def gram_cols():
+        for r, dev in ((3, xr), (1, xl), (2, xo)):
+            recv(("gxi", r), xi.at[c, zl, (x + 4 - r) % 4], dev)
+        send("gzi", xi.at[c, zl], xi.at[c, zl], zo)
+
+    def gram_in_sib():
+        recv("gzi", xi.at[c, 1 - zl], zo)
+        send("gsi", xi.at[c], xi.at[c], sib)
+
+    def tz_in(slot):
+        recv(("tz", slot), tpiece(slot, 1, x), zlp)
+        t_to_x(slot, 1)
 
     recv("tb", tpiece(1, 0, x), yb)
     t_to_x(1, 0)
@@ -219,27 +240,19 @@
     w_mid(0, 1)
     t_to_z(0)
     t_to_z(1)
-    for r, dev in ((3, xr), (1, xl), (2, xo)):
-        recv(("gxi", r), xi.at[c, zl, (x + 4 - r) % 4], dev)
-    send("gzi", xi.at[c, zl], xi.at[c, zl], zo)
+    gram_cols()
     t_from_x(1, 0)
     w_opp(0, 0)
     w_opp(0, 1)
     w_own(1, 0)
-    recv(("tz", 0), tpiece(0, 1, x), zlp)
-    t_to_x(0, 1)
-    recv(("tz", 1), tpiece(1, 1, x), zlp)
-    t_to_x(1, 1)
+    tz_in(0)
+    tz_in(1)
     w_own(1, 1)
     t_from_x(0, 1)
-    recv("gzi", xi.at[c, 1 - zl], zo)
-    send("gsi", xi.at[c], xi.at[c], sib)
     w_mid(1, 0)
     t_from_x(1, 1)
-    for r, dev in ((1, xr), (3, xl), (2, xo)):
-        send(("gxo", r), ghalf.at[:, o_cols((x + r) % 4)], xo_buf.at[c, zl, x], dev)
-
-    recv("gsi", xi.at[1 - c], sib)
+    gram_in_sib()
+
     my_cols = pl.ds(pl.multiple_of((zl * 2 + c) * kc, kc), kc)
 
     def gram(a, ref):
@@ -251,7 +264,6 @@
         for q in range(2):
             gbs[a, q] = gp[a, yy_of(1 - half, q)].astype(BF)
 
-    gram(0, xi)
     w_mid(1, 1)
     t_from_opp(0, 0)
     t_from_opp(1, 0)
@@ -259,6 +271,8 @@
     t_from_opp(1, 1)
     w_opp(1, 0)
     w_opp(1, 1)
+    recv("gsi", xi.at[1 - c], sib)
+    gram(0, xi)
     for r, dev in ((3, xr), (1, xl), (2, xo)):
         recv(("gxo", r), xo_buf.at[c, zl, (x + 4 - r) % 4], dev)
     send("gzo", xo_buf.at[c, zl], xo_buf.at[c, zl], zlp)
@@ -276,8 +290,8 @@
 
     def down(r, q):
         cols = pl.ds(pl.multiple_of((zz(r) * 2 + q) * kc, kc), kc)
-        acc = jnp.dot(ht[0], tok[0, :, :, :, :, cols].reshape(n_tok, kc), preferred_element_type=F32)
-        acc += jnp.dot(ht[1], tok[1, :, :, :, :, cols].reshape(n_tok, kc), preferred_element_type=F32)
+        acc = jnp.dot(ht[0, :hd, :], tok[0, :, :, :, :, cols].reshape(n_tok, kc), preferred_element_type=F32)
+        acc += jnp.dot(ht[1, :hd, :], tok[1, :, :, :, :, cols].reshape(n_tok, kc), preferred_element_type=F32)
         return acc * scale
 
     def dpiece(ref, i, p):
@@ -285,6 +299,32 @@
 
     def down_to_a(r, p):
         send(("da", r, p), dpiece(asnd, r, p), dpiece(arcv, r, p), ya)
+
+    def first_rows():
+        acc = jnp.dot(ht[0, hd:, :], tok[0].reshape(n_tok, kc * 8), preferred_element_type=F32)
+        acc += jnp.dot(ht[1, hd:, :], tok[1].reshape(n_tok, kc * 8), preferred_element_type=F32)
+        for j in range(8):
+            fp[j] = acc[:, j * kc:(j + 1) * kc] * scale
+        for q in range(2):
+            fs1[q] = fp[zz(2) * 2 + q].astype(BF)
+            send(("f1", q), fs1.at[q], f1.at[q], zr if q == 0 else zb)
+
+    def first_rows_2():
+        for q in range(2):
+            recv(("f1", q), f1.at[q], zb if q == 0 else zr)
+            r = 1 if q == 0 else 3
+            fs2[q, q] = (fp[zz(r) * 2 + q] + f1[q].astype(F32)).astype(BF)
+            fs2[q, 1 - q] = fp[zz(r) * 2 + 1 - q].astype(BF)
+            send(("f2", q), fs2.at[q], f2.at[q], zr if q == 0 else zb)
+
+    def first_sum(q):
+        return fp[zh * 2 + q] + f2[0, q].astype(F32) + f2[1, q].astype(F32)
+
+    def first_rows_to_a():
+        recv(("f2", 0), f2.at[0], zb)
+        recv(("f2", 1), f2.at[1], zr)
+        fas[...] = first_sum(1 - s).astype(BF)
+        send("fa", fas, far, ya)
 
     n_tile = n_tok // 2
 
@@ -298,16 +338,18 @@
         snd, rcv = (snd0, snd1)[hh], (rcv0, rcv1)[hh]
         send(("gh", hh, i), snd.at[at, :], rcv.at[at, :], yb)
 
+    asnd[2] = down(2, 1 - s).astype(BF)
+    down_to_a(2, 0)
+    down_to_a(2, 1)
+    first_rows()
     w_from_a(0)
     for i in range(2):
         snd0[i * n_tile:(i + 1) * n_tile, :] = hidden_grad(1, 0, i).astype(BF)
         hidden_to_b(0, i)
-    asnd[2] = down(2, 1 - s).astype(BF)
-    down_to_a(2, 0)
-    down_to_a(2, 1)
     asnd[1] = down(1, 1 - s).astype(BF)
     asnd[3] = down(3, 1 - s).astype(BF)
     part[2] = down(2, s)
+    first_rows_2()
     w_from_a(1)
     for i in range(2):
         snd1[i * n_tile:(i + 1) * n_tile, :] = hidden_grad(1, 1, i).astype(BF)
@@ -370,6 +412,7 @@
     send(("z1", 1), zs.at[1], z1.at[1], zb)
     down_to_a(1, 0)
     down_to_a(3, 1)
+    first_rows_to_a()
     gram_z1(0)
     part[1] = down(1, s)
     part[3] = down(3, s)
@@ -424,6 +467,11 @@
     finish(1)
     gram_out(1, go_ref, go_hbm)
 
+    last = pl.ds(hd, FIRST)
+    recv("fa", far, ya)
+    gd_ref[last, :] = (first_sum(s) + far[...].astype(F32)).astype(BF)
+    store(gd_ref.at[last, :], gd_hbm.at[last, :])
+
     for p in range(2):
         at = pl.ds(p * hf, hf)
         recv(("z2r", p), dpiece(z2, 0, p), zb)
@@ -439,11 +487,34 @@
     assert len(names) <= N_SEM and len(stores) <= 16, (len(names), len(stores))
 
 
+PARTS = 4
+
+
+def hand_over(*refs):
+    ins, outs = [], []
+    for i in range(5):
+        src, dst, mid = refs[i], refs[5 + i], refs[10 + i]
+        parts = PARTS if i < 3 else 1
+        n = src.shape[0] // parts
+        for p in range(parts):
+            at = pl.ds(p * n, n)
+            ins.append(pltpu.make_async_copy(src.at[at, :], mid.at[at, :], refs[15].at[i, p]))
+            outs.append(pltpu.make_async_copy(mid.at[at, :], dst.at[at, :], refs[16].at[i, p]))
+    for cp in ins:
+        cp.start()
+    for cp, out in zip(ins, outs):
+        cp.wait()
+        out.start()
+    for cp in outs:
+        cp.wait()
+
+
 def shards(x_rows, grad_out, gate_pre, up_pre, down_weight):
     rows, width = x_rows.shape
     n_tok, ffl = gate_pre.shape
     kc = down_weight.shape[1]
-    hf = ffl // 2
+    hd = ffl - FIRST
+    hf = hd // 2
     total = float(rows * lax.axis_size("tensor") * lax.axis_size("dp"))
     gr = kc // 16
     hbm = pl.BlockSpec(memory_space=pl.ANY)
@@ -458,7 +529,7 @@
         ((gr, BLOCK), F32),
         ((gr, BLOCK), F32),
     ]
-    return pl.pallas_call(
+    results = pl.pallas_call(
         kern,
         out_shape=tuple(jax.ShapeDtypeStruct(*o) for o in outs),
         in_specs=[hbm] * 5,
@@ -478,12 +549,19 @@
             pltpu.VMEM((2, 2, 4, rows, BLOCK), BF),
             pltpu.VMEM((2, 2, 4, rows, 2 * kc), BF),
             pltpu.VMEM((2, 2, 4, rows, BLOCK), BF),
-            pltpu.VMEM((4, ffl, kc), BF),
-            pltpu.VMEM((4, ffl, kc), BF),
-            pltpu.VMEM((4, ffl, kc), F32),
+            pltpu.VMEM((4, hd, kc), BF),
+            pltpu.VMEM((4, hd, kc), BF),
+            pltpu.VMEM((4, hd, kc), F32),
             pltpu.VMEM((6, hf, kc), BF),
             pltpu.VMEM((2, hf, kc), BF),
-            pltpu.VMEM((2, ffl, kc), BF),
+            pltpu.VMEM((2, hd, kc), BF),
+            pltpu.VMEM((8, FIRST, kc), F32),
+            pltpu.VMEM((2, FIRST, kc), BF),
+            pltpu.VMEM((2, 2, FIRST, kc), BF),
+            pltpu.VMEM((2, FIRST, kc), BF),
+            pltpu.VMEM((2, 2, FIRST, kc), BF),
+            pltpu.VMEM((FIRST, kc), BF),
+            pltpu.VMEM((FIRST, kc), BF),
             pltpu.VMEM((n_tok, SPLIT), BF),
             pltpu.VMEM((n_tok, ffl - SPLIT), BF),
             pltpu.VMEM((n_tok, SPLIT), BF),
@@ -510,6 +588,18 @@
             flops=4 * n_tok * width * ffl, bytes_accessed=8 * n_tok * ffl, transcendentals=0
         ),
     )(x_rows, grad_out, gate_pre, up_pre, down_weight)
+    return pl.pallas_call(
+        hand_over,
+        out_shape=tuple(jax.ShapeDtypeStruct(*o) for o in outs),
+        in_specs=[hbm] * 5,
+        out_specs=(hbm,) * 5,
+        scratch_shapes=[
+            *(pltpu.VMEM(*o) for o in outs),
+            pltpu.SemaphoreType.DMA((5, PARTS)),
+            pltpu.SemaphoreType.DMA((5, PARTS)),
+        ],
+        compiler_params=pltpu.CompilerParams(vmem_limit_bytes=60 * 1024 * 1024),
+    )(*results)
 
 
 def solution(mesh):

time: 117 us -> 110 us (0.940)
  the two profiles are of different devices: /device:TPU:1 before, /device:TPU:38 now
where the time goes in v3:
time: 110 us
  Pallas kernels  109 us (99%)
    pallas_call x1, Pallas kernels, shards(): pl.pallas_call(kern, out_shape=tuple((jax.ShapeDtypeStruct(*o) for o in o...  106 us
    pallas_call x1, Pallas kernels, shards(): pl.pallas_call(hand_over, out_shape=tuple((jax.ShapeDtypeStruct(*o) for o...  3.04 us

profile of v3, /device:TPU:38, one launch (start us, length us, event | category | flops | bytes accessed | tf_op | source)
XLA Modules:
  0.0 110.0 jit_solution(2753523346655109313)
XLA Ops:
  0.6 106.3 %shard_map.92 = (bf16[768,896]{1,0:T(8,128)(2,1)}, bf16[768,896]{1,0:T(8,128)(2,1)}, bf16[896,256]{1,0:T(8,128)(2,1)}, f32[16,1024]{1,0:T(8,128)}, f32[16,1024]{1,0:T(8,128)}) custom-call(bf16[48,4096]{1,0:T(8,128)(2,1)} %refs_0_.1, bf16[48,4096]{1,0:T(8,128)(2,1)} %refs_1_.1, bf16[768,896]{1,0:T(8,128)(2,1)} %refs_2_.1, bf16[768,896]{1,0:T(8,128)(2,1)} %refs_3_.1, ...), custom_call_target="tpu_custom_call" | custom-call | flops 11274289152 | bytes 5505024 | tf_op jit(solution)/shard_map/pallas_call | solution.py:532
  106.9 3.0 %shard_map.93 = (bf16[768,896]{1,0:T(8,128)(2,1)}, bf16[768,896]{1,0:T(8,128)(2,1)}, bf16[896,256]{1,0:T(8,128)(2,1)}, f32[16,1024]{1,0:T(8,128)}, f32[16,1024]{1,0:T(8,128)}) custom-call(bf16[768,896]{1,0:T(8,128)(2,1)} %get-tuple-element.10.refs_0_, bf16[768,896]{1,0:T(8,128)(2,1)} %get-tuple-element.11.refs_1_, ...), custom_call_target="tpu_custom_call" | custom-call | tf_op jit(solution)/shard_map/pallas_call | solution.py:591

commit v4 on v3

--- a/solution.py
+++ b/solution.py
@@ -13,7 +13,7 @@
 BLOCK = 1024
 N_SEM = 128
 SPLIT = 512
-FIRST = 128
+FIRST = 160
 
 
 def kernel(
@@ -237,8 +237,8 @@
     t_to_x(1, 0)
     w_mid(0, 0)
     t_from_x(0, 0)
+    t_to_z(0)
     w_mid(0, 1)
-    t_to_z(0)
     t_to_z(1)
     gram_cols()
     t_from_x(1, 0)
@@ -265,6 +265,9 @@
             gbs[a, q] = gp[a, yy_of(1 - half, q)].astype(BF)
 
     w_mid(1, 1)
+    for r, dev in ((3, xr), (1, xl), (2, xo)):
+        recv(("gxo", r), xo_buf.at[c, zl, (x + 4 - r) % 4], dev)
+    send("gzo", xo_buf.at[c, zl], xo_buf.at[c, zl], zlp)
     t_from_opp(0, 0)
     t_from_opp(1, 0)
     t_from_opp(0, 1)
@@ -273,9 +276,6 @@
     w_opp(1, 1)
     recv("gsi", xi.at[1 - c], sib)
     gram(0, xi)
-    for r, dev in ((3, xr), (1, xl), (2, xo)):
-        recv(("gxo", r), xo_buf.at[c, zl, (x + 4 - r) % 4], dev)
-    send("gzo", xo_buf.at[c, zl], xo_buf.at[c, zl], zlp)
     for p in range(2):
         cols = pl.ds(p * n_tok // 2, n_tok // 2)
         recv(("h", p), ht.at[1, :, cols], yb)

time: 110 us -> 108 us (0.982)
  the two profiles are of different devices: /device:TPU:38 before, /device:TPU:1 now
where the time goes in v4:
time: 108 us
  Pallas kernels  108 us (100%)
    pallas_call x1, Pallas kernels, shards(): pl.pallas_call(kern, out_shape=tuple((jax.ShapeDtypeStruct(*o) for o in o...  105 us
    pallas_call x1, Pallas kernels, shards(): pl.pallas_call(hand_over, out_shape=tuple((jax.ShapeDtypeStruct(*o) for o...  3.04 us

profile of v4, /device:TPU:1, one launch (start us, length us, event | category | flops | bytes accessed | tf_op | source)
XLA Modules:
  0.0 108.4 jit_solution(14179737947703922211)
XLA Ops:
  0.6 104.7 %shard_map.92 = (bf16[768,896]{1,0:T(8,128)(2,1)}, bf16[768,896]{1,0:T(8,128)(2,1)}, bf16[896,256]{1,0:T(8,128)(2,1)}, f32[16,1024]{1,0:T(8,128)}, f32[16,1024]{1,0:T(8,128)}) custom-call(bf16[48,4096]{1,0:T(8,128)(2,1)} %refs_0_.1, bf16[48,4096]{1,0:T(8,128)(2,1)} %refs_1_.1, bf16[768,896]{1,0:T(8,128)(2,1)} %refs_2_.1, bf16[768,896]{1,0:T(8,128)(2,1)} %refs_3_.1, ...), custom_call_target="tpu_custom_call" | custom-call | flops 11274289152 | bytes 5505024 | tf_op jit(solution)/shard_map/pallas_call | solution.py:532
  105.4 3.0 %shard_map.93 = (bf16[768,896]{1,0:T(8,128)(2,1)}, bf16[768,896]{1,0:T(8,128)(2,1)}, bf16[896,256]{1,0:T(8,128)(2,1)}, f32[16,1024]{1,0:T(8,128)}, f32[16,1024]{1,0:T(8,128)}) custom-call(bf16[768,896]{1,0:T(8,128)(2,1)} %get-tuple-element.10.refs_0_, bf16[768,896]{1,0:T(8,128)(2,1)} %get-tuple-element.11.refs_1_, ...), custom_call_target="tpu_custom_call" | custom-call | tf_op jit(solution)/shard_map/pallas_call | solution.py:591

commit v5 on v4

--- a/solution.py
+++ b/solution.py
@@ -13,7 +13,7 @@
 BLOCK = 1024
 N_SEM = 128
 SPLIT = 512
-FIRST = 160
+FIRST = 192
 
 
 def kernel(

time: 108 us -> 110 us (1.019)
    pallas_call x1, Pallas kernels: 105 us -> 106 us  [shards(): pl.pallas_call(kern, out_shape=tuple((jax.ShapeDtypeStruct(*o) for o in o...]
where the time goes in v5:
time: 110 us
  Pallas kernels  109 us (99%)
    pallas_call x1, Pallas kernels, shards(): pl.pallas_call(kern, out_shape=tuple((jax.ShapeDtypeStruct(*o) for o in o...  106 us
    pallas_call x1, Pallas kernels, shards(): pl.pallas_call(hand_over, out_shape=tuple((jax.ShapeDtypeStruct(*o) for o...  3.04 us

profile of v5, /device:TPU:1, one launch (start us, length us, event | category | flops | bytes accessed | tf_op | source)
XLA Modules:
  0.0 109.7 jit_solution(12708404700632390996)
XLA Ops:
  0.6 105.8 %shard_map.92 = (bf16[768,896]{1,0:T(8,128)(2,1)}, bf16[768,896]{1,0:T(8,128)(2,1)}, bf16[896,256]{1,0:T(8,128)(2,1)}, f32[16,1024]{1,0:T(8,128)}, f32[16,1024]{1,0:T(8,128)}) custom-call(bf16[48,4096]{1,0:T(8,128)(2,1)} %refs_0_.1, bf16[48,4096]{1,0:T(8,128)(2,1)} %refs_1_.1, bf16[768,896]{1,0:T(8,128)(2,1)} %refs_2_.1, bf16[768,896]{1,0:T(8,128)(2,1)} %refs_3_.1, ...), custom_call_target="tpu_custom_call" | custom-call | flops 11274289152 | bytes 5505024 | tf_op jit(solution)/shard_map/pallas_call | solution.py:532
  106.5 3.0 %shard_map.93 = (bf16[768,896]{1,0:T(8,128)(2,1)}, bf16[768,896]{1,0:T(8,128)(2,1)}, bf16[896,256]{1,0:T(8,128)(2,1)}, f32[16,1024]{1,0:T(8,128)}, f32[16,1024]{1,0:T(8,128)}) custom-call(bf16[768,896]{1,0:T(8,128)(2,1)} %get-tuple-element.10.refs_0_, bf16[768,896]{1,0:T(8,128)(2,1)} %get-tuple-element.11.refs_1_, ...), custom_call_target="tpu_custom_call" | custom-call | tf_op jit(solution)/shard_map/pallas_call | solution.py:591
